TPU v7x, 512 devices: a whole 4x8x8 slice. The times are simulated.
512 devices in a mesh: fsdp: 64 (over y, z_hi, core), tp: 8 (over x, z_lo).
Axes of the slice: x: 4, y: 8, z: 8 (z_hi: 4, z_lo: 2; z = z_hi * 2 + z_lo), core: 2. Of those that a mesh axis runs over, the one named last changes fastest.
Arguments:
- tokens: bfloat16 [8192, 4096], P('fsdp'), may hold values from -16 to 16
- gate_pre: bfloat16 [8192, 14784], P('fsdp', 'tp'), may hold values from -8 to 8
- hid_grad: bfloat16 [8192, 14784], P('fsdp', 'tp'), may hold values from -6 to 6
- up_weight: bfloat16 [4096, 14784], P('fsdp', 'tp'), may hold values from -0.046875 to 0.046875
- grad_accum: float32 [4096, 14784], P('fsdp', 'tp'), may hold values from -6 to 6
Outputs:
- weight_grad: float32 [4096, 14784], P('fsdp', 'tp')
- input_grad: bfloat16 [8192, 4096], P('fsdp', 'tp')
All inputs are finite; a program needn't handle non-finite values.
Results may differ from a plain program's by a relative error of at most 0.017.
Values may be sent and summed in bfloat16 or wider, within the bound.
A program may use at most 192 MiB of HBM per device.

v0:
```python
import math

import jax
import jax.numpy as jnp
from jax import lax
from jax.sharding import PartitionSpec as P


def on_device(tokens, gate_pre, hid_grad, up_weight, grad_accum):
    up_grad = (hid_grad.astype(jnp.float32) * jax.nn.silu(gate_pre.astype(jnp.float32))).astype(
        jnp.bfloat16
    )
    norm_factor = 1.0 / math.sqrt(tokens.shape[0] * lax.axis_size("fsdp"))
    partial_value = lax.dot_general(
        up_grad,
        lax.all_gather(up_weight, "fsdp", axis=0, tiled=True),
        (((1,), (1,)), ((), ())),
        preferred_element_type=jnp.float32,
    ).astype(jnp.bfloat16)
    partial_value = partial_value.astype(jnp.float32)
    summed_input = lax.psum(partial_value.astype(jnp.bfloat16), "tp").astype(jnp.float32)
    own_columns = partial_value.shape[1] // lax.axis_size("tp")
    summed_input = lax.dynamic_slice_in_dim(
        summed_input, lax.axis_index("tp") * own_columns, own_columns, 1
    )
    input_grad = summed_input.astype(jnp.bfloat16)
    complete = lax.dot_general(
        tokens, up_grad, (((0,), (0,)), ((), ())), preferred_element_type=jnp.float32
    )
    summed_grad = lax.psum_scatter(complete, "fsdp", scatter_dimension=0, tiled=True)
    weight_grad = grad_accum + summed_grad * norm_factor
    return (weight_grad, input_grad)


def solution(mesh):
    in_specs = (P("fsdp", None), P("fsdp", "tp"), P("fsdp", "tp"), P("fsdp", "tp"), P("fsdp", "tp"))
    out_specs = (P("fsdp", "tp"), P("fsdp", "tp"))
    return jax.shard_map(
        on_device, mesh=mesh, in_specs=in_specs, out_specs=out_specs, check_vma=False
    )
```

profile of v0, /device:TPU:1, one launch (start us, length us, event | category | flops | bytes accessed | tf_op | source)
XLA Modules:
  0.0 562.1 jit_solution(13335248015391063661)
XLA Ops:
  7.2 0.0 copy-start
  7.2 0.0 copy-start.2
  7.2 0.0 copy-start.3
  7.2 0.0 all-gather.2.cloned.1.call-start
  7.2 0.7 all-gather.2.cloned.1.call-update
  7.9 0.0 all-reduce.2.cloned.1.call-start
  8.0 145.9 %all-gather.2.cloned.1.call-done = bf16[4096,1848]{1,0:T(8,128)(2,1)} async-done(((bf16[64,1848]{1,0:T(8,128)(2,1)}), bf16[4096,1848]{1,0:T(8,128)(2,1)}) %all-gather.2.cloned.1.call-update) | async-done | bytes 15138832 | tf_op jit(solution)/shard_map/all_gather | solution.py:16
  153.9 12.0 %convolution_convert_fusion = bf16[128,4096]{1,0:T(8,128)(2,1)} fusion(bf16[4096,1848]{1,0:T(8,128)(2,1)} %all-gather.2.cloned.1.call-done, bf16[128,1848]{0,1:T(8,128)(2,1)} %param.6, bf16[128,1848]{0,1:T(8,128)(2,1)} %param.7), kind=kOutput, calls=%fused_computation.1 | convolution fusion | flops 1940185088 | bytes 17133568 | tf_op jit(solution)/shard_map/dot_general | solution.py:14
  165.9 0.0 all-reduce.2.cloned.1.call-update
  165.9 0.0 reduce-scatter.4.cloned.1.call-start
  166.0 0.0 copy-done
  166.0 0.0 copy-done.2
  166.0 0.0 copy-done.3
  166.0 12.1 %convolution_bitcast_fusion = f32[4096,1848]{0,1:T(8,128)} fusion(bf16[128,4096]{1,0:T(8,128)(2,1)S(1)} %copy-done, bf16[128,1848]{0,1:T(8,128)(2,1)S(1)} %copy-done.2, bf16[128,1848]{0,1:T(8,128)(2,1)S(1)} %copy-done.3), kind=kOutput, calls=%fused_computation | convolution fusion | flops 1939660800 | bytes 32272384 | tf_op jit(solution)/shard_map/dot_general | solution.py:27
  178.1 30.6 %copy.11 = f32[4096,1848]{1,0:T(8,128)} copy(f32[4096,1848]{0,1:T(8,128)} %convolution_bitcast_fusion) | data formatting | bytes 60555264
  208.7 0.0 copy-start.1
  208.7 0.0 copy-start.4
  208.7 0.0 reduce-scatter.4.cloned.1.call-update
  208.7 1.1 copy-done.4
  209.8 0.3 copy.9
  210.1 37.9 %all-reduce.2.cloned.1.call-done = bf16[128,4096]{1,0:T(8,128)(2,1)} async-done(((bf16[128,4096]{1,0:T(8,128)(2,1)}), bf16[128,4096]{1,0:T(8,128)(2,1)}) %all-reduce.2.cloned.1.call-update) | async-done | bytes 1048592 | tf_op jit(solution)/shard_map/psum | solution.py:21
  248.0 1.6 convert_convert_fusion
  249.5 301.3 %reduce-scatter.4.cloned.1.call-done = f32[64,1848]{1,0:T(8,128)} async-done(((f32[4096,1848]{1,0:T(8,128)}), f32[64,1848]{1,0:T(8,128)}) %reduce-scatter.4.cloned.1.call-update) | async-done | bytes 473104
  550.9 1.3 copy.12
  552.2 1.1 multiply_add_fusion
  553.3 2.3 copy.10
  555.6 0.0 copy-done.1
Async XLA Ops:
  7.2 158.8 %copy-start = (bf16[128,4096]{1,0:T(8,128)(2,1)S(1)}, bf16[128,4096]{1,0:T(8,128)(2,1)}, u32[]{:S(2)}) copy-start(bf16[128,4096]{1,0:T(8,128)(2,1)} %param.5) | copy-start | bytes 3145732
  7.2 158.8 %copy-start.2 = (bf16[128,1848]{0,1:T(8,128)(2,1)S(1)}, bf16[128,1848]{0,1:T(8,128)(2,1)}, u32[]{:S(2)}) copy-start(bf16[128,1848]{0,1:T(8,128)(2,1)} %param.6) | copy-start | bytes 1419268
  7.2 158.8 %copy-start.3 = (bf16[128,1848]{0,1:T(8,128)(2,1)S(1)}, bf16[128,1848]{0,1:T(8,128)(2,1)}, u32[]{:S(2)}) copy-start(bf16[128,1848]{0,1:T(8,128)(2,1)} %param.7) | copy-start | bytes 1419268
  7.2 146.6 %all-gather.2.cloned.1.call-start = ((), (), s32[]{:S(2)}) async-start(), calls=%async_computation.1 | async-start | bytes 15974400 | tf_op jit(solution)/shard_map/all_gather | solution.py:16
  7.9 240.0 %all-reduce.2.cloned.1.call-start = ((), (), s32[]{:S(2)}) async-start(), calls=%async_computation.2 | async-start | bytes 2097152 | tf_op jit(solution)/shard_map/psum | solution.py:21
  165.9 385.0 %reduce-scatter.4.cloned.1.call-start = ((), (), s32[]{:S(2)}) async-start(), calls=%async_computation.3 | async-start | bytes 31948800
  208.7 347.0 %copy-start.1 = (bf16[128,4096]{1,0:T(8,128)(2,1)S(1)}, bf16[128,4096]{1,0:T(8,128)(2,1)}, u32[]{:S(2)}) copy-start(bf16[128,4096]{1,0:T(8,128)(2,1)} %param.5) | copy-start | bytes 3145732
  208.7 1.1 copy-start.4
Sparse Core Ops, SparseCore 0:
  11.3 142.4 all-gather.1
  166.0 81.9 all-reduce.1
  253.3 297.5 reduce-scatter.3
where the time goes:
time: 566 us; the launch traced here: 562 us
  waiting for transfers between devices  486 us (86%)
  local copies, waits for them, and re-layouts  35.6 us (6%)
  matrix products  24.1 us (4%)
  between operations  13.8 us (2%)
    unnamed x4, waiting for transfers between devices  302 us
    all_gather x1, waiting for transfers between devices, on_device(): lax.all_gather(up_weight, 'fsdp', axis=0, tiled=True)  146 us
    psum x1, waiting for transfers between devices, on_device(): lax.psum(partial_value.astype(jnp.bfloat16), 'tp').astype(jnp.float32)  37.9 us
    unnamed x14, local copies, waits for them, and re-layouts  35.6 us
    dot_general x1, matrix products, on_device(): lax.dot_general(tokens, up_grad, (((0,), (0,)), ((), ())), preferred_elem...  12.1 us
    dot_general x1, matrix products, on_device(): lax.dot_general(up_grad, lax.all_gather(up_weight, 'fsdp', axis=0, tiled=...  12 us
  transfers between devices with their start and end apart: 3, of which 3 were waited for; matrix products, arithmetic and copies ran while one was open for 8% of the time, Pallas kernels for 0%

commit v1 on v0

v1 whole, which is shorter than its diff:
```python
import math

import jax
import jax.numpy as jnp
from jax import lax
from jax.sharding import Mesh, PartitionSpec as P


def on_device(tokens, gate_pre, hid_grad, up_weight, grad_accum):
    up_grad = (hid_grad.astype(jnp.float32) * jax.nn.silu(gate_pre.astype(jnp.float32))).astype(
        jnp.bfloat16
    )
    n_y, n_zc, n_tp = (lax.axis_size(a) for a in ("y", "zc", "tp"))
    norm_factor = 1.0 / math.sqrt(tokens.shape[0] * n_y * n_zc)
    rows, channels = tokens.shape
    block = channels // n_y
    tok = lax.all_to_all(tokens.reshape(rows, n_y, block), "y", 1, 0, tiled=True)
    tok = tok.reshape(rows * n_y, block)
    ups = lax.all_gather(up_grad, "y", axis=0, tiled=True)
    weight = lax.all_gather(up_weight, "zc", axis=0, tiled=True)
    partial_value = lax.dot_general(
        ups, weight, (((1,), (1,)), ((), ())), preferred_element_type=jnp.float32
    ).astype(jnp.bfloat16)
    summed_input = lax.psum_scatter(partial_value, "tp", scatter_dimension=0, tiled=True)
    input_grad = lax.ppermute(
        summed_input,
        ("y", "tp"),
        [(y * n_tp + t, t * n_tp + y) for y in range(n_y) for t in range(n_tp)],
    )
    complete = lax.dot_general(
        tok, ups, (((0,), (0,)), ((), ())), preferred_element_type=jnp.float32
    ).astype(jnp.bfloat16)
    summed_grad = lax.psum_scatter(complete, "zc", scatter_dimension=0, tiled=True)
    weight_grad = grad_accum + summed_grad.astype(jnp.float32) * norm_factor
    return (weight_grad, input_grad)


def solution(mesh):
    fine = Mesh(mesh.devices.reshape(8, 8, 8), ("y", "zc", "tp"))
    rows, both = P(("y", "zc"), None), P(("y", "zc"), "tp")
    return jax.shard_map(
        on_device,
        mesh=fine,
        in_specs=(rows, both, both, both, both),
        out_specs=(both, both),
        check_vma=False,
    )
```

time: 566 us -> 225 us (0.40)
  waiting for transfers between devices: 486 us -> 180 us
  local copies, waits for them, and re-layouts: 35.6 us -> 8.57 us
  matrix products: 24.1 us -> 10.3 us
  starting transfers between devices: 0.12 us -> 9.36 us
    unnamed x4 -> x5, waiting for transfers between devices: 302 us -> 49.4 us
    all_gather x1 -> x2, waiting for transfers between devices: 146 us -> 93.3 us  [the longest x1 59.1 us: on_device(): ups = lax.all_gather(up_grad, 'y', axis=0, tiled=True)]
    psum x1 -> x0, waiting for transfers between devices: 37.9 us -> none  [on_device(): lax.psum(partial_value.astype(jnp.bfloat16), 'tp').astype(jnp.float32)]
    reduce_scatter x0 -> x1, waiting for transfers between devices: none -> 36.8 us  [on_device(): lax.psum_scatter(partial_value, 'tp', scatter_dimension=0, tiled=True)]
    unnamed x14 -> x8, local copies, waits for them, and re-layouts: 35.6 us -> 8.04 us
    dot_general x2, matrix products: 24.1 us -> 10.3 us  [the longest x1 6.09 us: on_device(): lax.dot_general(ups, weight, (((1,), (1,)), ((), ())), preferred_element_...]
    all_to_all x0 -> x1, starting transfers between devices: none -> 7.65 us  [on_device(): lax.all_to_all(tokens.reshape(rows, n_y, block), 'y', 1, 0, tiled=True)]
  transfers between devices with their start and end apart: 3 -> 6, of which waited for: 3 -> 4; matrix products, arithmetic and copies ran while one was open for 8% -> 8% of each run, Pallas kernels for 0% -> 0%
where the time goes in v1:
time: 225 us; the launch traced here: 224 us
  waiting for transfers between devices  180 us (80%)
  between operations  13.8 us (6%)
  matrix products  10.3 us (5%)
  starting transfers between devices  9.36 us (4%)
  local copies, waits for them, and re-layouts  8.57 us (4%)
  other arithmetic  2.34 us (1%)
    all_gather x1, waiting for transfers between devices, on_device(): ups = lax.all_gather(up_grad, 'y', axis=0, tiled=True)  59.1 us
    unnamed x5, waiting for transfers between devices  49.4 us
    reduce_scatter x1, waiting for transfers between devices, on_device(): lax.psum_scatter(partial_value, 'tp', scatter_dimension=0, tiled=True)  36.8 us
    all_gather x1, waiting for transfers between devices, on_device(): weight = lax.all_gather(up_weight, 'zc', axis=0, tiled=True)  34.1 us
    unnamed x8, local copies, waits for them, and re-layouts  8.04 us
    all_to_all x1, starting transfers between devices, on_device(): lax.all_to_all(tokens.reshape(rows, n_y, block), 'y', 1, 0, tiled=True)  7.65 us
    dot_general x1, matrix products, on_device(): lax.dot_general(ups, weight, (((1,), (1,)), ((), ())), preferred_element_...  6.09 us
  transfers between devices with their start and end apart: 6, of which 4 were waited for; matrix products, arithmetic and copies ran while one was open for 8% of the time, Pallas kernels for 0%

profile of v1, /device:TPU:1, one launch (start us, length us, event | category | flops | bytes accessed | tf_op | source)
XLA Modules:
  0.0 223.9 jit_solution(1652158043575437935)
XLA Ops:
  7.2 0.0 all-gather.5.cloned.1.call-start
  7.2 0.7 all-gather.5.cloned.1.call-update
  7.9 0.0 all-gather.3.cloned.1.call-start
  7.9 2.2 fusion.5
  10.2 0.0 all-gather.3.cloned.1.call-update
  10.2 2.3 %copy.15 = bf16[128,4096]{0,1:T(8,128)(2,1)} copy(bf16[128,4096]{1,0:T(8,128)(2,1)} %param.5) | data formatting | bytes 2097152 | tf_op args[0]
  12.5 7.7 %all-to-all-start = ((bf16[128,8,512]{0,2,1:T(8,128)(2,1)}), bf16[128,8,512]{0,2,1:T(8,128)(2,1)S(1)}, u32[]{:S(2)}, u32[]{:S(2)}) async-start(bf16[128,8,512]{0,2,1:T(8,128)(2,1)} %bitcast), calls=%async_computation | async-start | bytes 2097152 | tf_op jit(solution)/shard_map/all_to_all | solution.py:17
  20.1 0.0 reduce-scatter.5.cloned.1.call-start
  20.1 34.1 %all-gather.5.cloned.1.call-done = bf16[512,1848]{1,0:T(8,128)(2,1)} async-done(((bf16[64,1848]{1,0:T(8,128)(2,1)}), bf16[512,1848]{1,0:T(8,128)(2,1)}) %all-gather.5.cloned.1.call-update) | async-done | bytes 1892368 | tf_op jit(solution)/shard_map/all_gather | solution.py:20
  54.3 59.1 %all-gather.3.cloned.1.call-done = bf16[1024,1848]{0,1:T(8,128)(2,1)} async-done(((bf16[128,1848]{0,1:T(8,128)(2,1)}), bf16[1024,1848]{0,1:T(8,128)(2,1)}) %all-gather.3.cloned.1.call-update) | async-done | bytes 3784720 | tf_op jit(solution)/shard_map/all_gather | solution.py:19
  113.4 6.1 %convolution_convert_fusion.1 = bf16[1024,512]{1,0:T(8,128)(2,1)} fusion(bf16[1024,1848]{0,1:T(8,128)(2,1)} %all-gather.3.cloned.1.call-done, bf16[512,1848]{1,0:T(8,128)(2,1)} %all-gather.5.cloned.1.call-done), kind=kOutput, calls=%fused_computation.2 | convolution fusion | flops 1938292736 | bytes 6725632 | tf_op jit(solution)/shard_map/dot_general | solution.py:21
  119.5 0.0 reduce-scatter.5.cloned.1.call-update
  119.5 0.0 reduce-scatter.7.cloned.1.call-start
  119.6 0.0 all-to-all-done
  119.6 0.5 copy.16
  120.1 4.2 %fusion = bf16[512,1848]{0,1:T(8,128)(2,1)S(1)} fusion(bf16[1024,1848]{0,1:T(8,128)(2,1)} %all-gather.3.cloned.1.call-done, bf16[1024,512]{1,0:T(8,128)(2,1)S(1)} %bitcast.13), kind=kOutput, calls=%fused_computation.1 | convolution fusion | flops 1938714624 | bytes 6725632 | tf_op jit(solution)/shard_map/dot_general | solution.py:30
  124.4 0.0 copy-start
  124.4 2.5 %copy.19 = bf16[512,1848]{1,0:T(8,128)(2,1)} copy(bf16[512,1848]{0,1:T(8,128)(2,1)S(1)} %fusion) | data formatting | bytes 3784704
  126.9 0.0 reduce-scatter.7.cloned.1.call-update
  126.9 36.8 %reduce-scatter.5.cloned.1.call-done = bf16[128,512]{1,0:T(8,128)(2,1)} async-done(((bf16[1024,512]{1,0:T(8,128)(2,1)}), bf16[128,512]{1,0:T(8,128)(2,1)}) %reduce-scatter.5.cloned.1.call-update) | async-done | bytes 131088 | tf_op jit(solution)/shard_map/reduce_scatter | solution.py:24
  163.7 1.6 collective-permute-start
  165.3 0.0 copy-done
  165.3 0.3 copy.17
  165.6 0.0 collective-permute-done
  165.6 48.7 %reduce-scatter.7.cloned.1.call-done = bf16[64,1848]{1,0:T(8,128)(2,1)} async-done(((bf16[512,1848]{1,0:T(8,128)(2,1)}), bf16[64,1848]{1,0:T(8,128)(2,1)}) %reduce-scatter.7.cloned.1.call-update) | async-done | bytes 236560
  214.3 1.2 copy.20
  215.5 0.1 multiply_add_fusion
  215.6 1.1 copy.18
  216.7 0.7 copy.22
Async XLA Ops:
  7.2 47.1 %all-gather.5.cloned.1.call-start = ((), (), s32[]{:S(2)}) async-start(), calls=%async_computation.4 | async-start | bytes 2211840 | tf_op jit(solution)/shard_map/all_gather | solution.py:20
  7.9 105.5 %all-gather.3.cloned.1.call-start = ((), (), s32[]{:S(2)}) async-start(), calls=%async_computation.3 | async-start | bytes 4257792 | tf_op jit(solution)/shard_map/all_gather | solution.py:19
  12.5 107.1 %all-to-all-start = ((bf16[128,8,512]{0,2,1:T(8,128)(2,1)}), bf16[128,8,512]{0,2,1:T(8,128)(2,1)S(1)}, u32[]{:S(2)}, u32[]{:S(2)}) async-start(bf16[128,8,512]{0,2,1:T(8,128)(2,1)} %bitcast), calls=%async_computation | async-start | bytes 2097152 | tf_op jit(solution)/shard_map/all_to_all | solution.py:17
  20.1 143.6 %reduce-scatter.5.cloned.1.call-start = ((), (), s32[]{:S(2)}) async-start(), calls=%async_computation.5 | async-start | bytes 1179648 | tf_op jit(solution)/shard_map/reduce_scatter | solution.py:24
  119.5 94.8 %reduce-scatter.7.cloned.1.call-start = ((), (), s32[]{:S(2)}) async-start(), calls=%async_computation.6 | async-start | bytes 2211840
  124.4 40.9 %copy-start = (f32[64,1848]{1,0:T(8,128)S(1)}, f32[64,1848]{1,0:T(8,128)}, u32[]{:S(2)}) copy-start(f32[64,1848]{1,0:T(8,128)} %param.9) | copy-start | bytes 1419268
  163.7 1.9 collective-permute-start
Sparse Core Ops, SparseCore 0:
  10.1 44.1 all-gather.4
  56.9 56.5 all-gather.2
  119.7 44.0 reduce-scatter.4
  166.5 47.7 reduce-scatter.6

commit v2 on v1

v2 whole, which is shorter than its diff:
```python
import functools
import math

import jax
import jax.numpy as jnp
from jax import lax
from jax.experimental import pallas as pl
from jax.experimental.pallas import tpu as pltpu
from jax.sharding import Mesh, PartitionSpec as P

NY, NH, NC, NX, NL = 8, 4, 2, 4, 2
OFF = (0, 1, -1, 2, -2, 3, -3, 4)
BACK = (0, 2, 1, 4, 3, 6, 5, 7)
GROUPS = ((0, 1, 2), (3, 4), (5, 6), (7,))
F32, BF16 = jnp.float32, jnp.bfloat16


def chunks_of(width):
    starts = list(range(0, width, 512))
    return [(s, min(512, width - s)) for s in starts]


def kernel(norm, chunks, n_copies, tokens, gate, hid, w_own, accum, wg_out, ig_out, *scratch):
    scratch = list(scratch)
    take = lambda n: [scratch.pop(0) for _ in range(n)]
    nk = len(chunks)
    send_sem, recv_sem, fin_send, fin_recv = take(4)
    tok, tok_t, w_all, fin = take(4)
    up = take(nk)
    b_send, b_recv, b_own, b_sum = take(nk), take(nk), take(nk), take(nk)
    b_a, b_b, b_tp, b_tm, b_l, b_r = (take(nk) for _ in range(6))
    ng = len(GROUPS)
    p_all, p_a, p_b, p_tp, p_tm, p_l, p_r = (take(ng) for _ in range(7))
    p_sum, p_half, p_z, p_fin = (take(ng) for _ in range(4))

    y, zh, c, x, zl = (lax.axis_index(a) for a in ("y", "zh", "c", "x", "zl"))
    zc, t = zh * NC + c, x * NL + zl
    around = lambda v, n: lax.rem(v + n, n)
    y_up, y_down = {"y": around(y + 1, NY)}, {"y": around(y - 1, NY)}
    h_up, h_down = around(zh + 1, NH), around(zh - 1, NH)
    h_far = around(zh + 2, NH)
    x_up, x_down, x_far = around(x + 1, NX), around(x - 1, NX), around(x + 2, NX)
    sib, pair = {"c": 1 - c}, {"zl": 1 - zl}
    fin_x, fin_l = y // NL, lax.rem(y, NL)

    copies = []

    def send(src, dst, device):
        i = len(copies)
        copy = pltpu.make_async_remote_copy(
            src_ref=src,
            dst_ref=dst,
            send_sem=send_sem.at[i],
            recv_sem=recv_sem.at[i],
            device_id=device,
            device_id_type=pl.DeviceIdType.MESH,
        )
        copy.start()
        copies.append(copy)
        return copy

    def fin_copy(j, src, sem):
        return pltpu.make_async_remote_copy(
            src_ref=src,
            dst_ref=fin.at[x, zl],
            send_sem=fin_send.at[j],
            recv_sem=fin_recv.at[sem],
            device_id={"y": around(y + OFF[j], NY), "x": fin_x, "zl": fin_l},
            device_id_type=pl.DeviceIdType.MESH,
        )

    barrier = pltpu.get_barrier_semaphore()

    def greet(device):
        pl.semaphore_signal(
            barrier, inc=1, device_id=device, device_id_type=pl.DeviceIdType.MESH
        )

    for j in range(1, NY):
        greet({"y": around(y + OFF[j], NY)})
    for device in ({"zh": h_up}, {"zh": h_down}, {"x": x_up}, {"x": x_down}, sib, pair):
        greet(device)
    for other in range(NX * NL):

        @pl.when(jnp.logical_or(t != y, t != other))
        def _():
            greet({"y": t, "x": other // NL, "zl": other % NL})

    def up_grad(k):
        at, width = chunks[k]
        v = gate[:, at : at + width].astype(F32)
        g = hid[:, at : at + width].astype(F32)
        up[k][0] = (g * (v / (1.0 + jnp.exp(-v)))).astype(BF16)

    up_grad(0)
    pl.semaphore_wait(barrier, NY - 1 + 6 + jnp.where(t == y, NX * NL - 1, NX * NL))

    ring = {}
    PLUS, MINUS = (0, 2, 4, 6, 7), (0, 1, 3, 5, 7)

    def pass_on(k, s):
        for way, path, device in ((0, PLUS, y_up), (1, MINUS, y_down)):
            src, dst = up[k].at[path[s]], up[k].at[path[s + 1]]
            if s == 3:
                half = pl.ds(way * 64, 64)
                src, dst = src.at[half], dst.at[half]
            ring[k, s, way] = send(src, dst, device)

    def arrived(k, s):
        for way in (0, 1):
            ring[k, s - 1, way].wait_recv()

    pass_on(0, 0)

    tok_in = []
    for j in range(1, NY):
        to = around(y + OFF[j], NY)
        tok_in.append(
            send(
                tokens.at[
                    pl.ds(pl.multiple_of(x * 32, 32), 32), pl.ds(pl.multiple_of(to * 512, 512), 512)
                ],
                tok.at[BACK[j], x],
                {"y": to},
            )
        )
    w_in = [send(w_own, w_all.at[zc], device) for device in ({"zh": h_up}, {"zh": h_down}, sib)]

    up_grad(1)
    pass_on(1, 0)
    up_grad(2)
    up_grad(3)
    w_all[zc] = w_own[...]

    def w_forward():
        w_in[0].wait_recv()
        w_in[1].wait_recv()
        left, right = h_down * NC + c, h_up * NC + c
        a, b = pl.ds(0, 32), pl.ds(32, 32)
        w_in.append(send(w_all.at[left, a], w_all.at[left, a], {"zh": h_up}))
        w_in.append(send(w_all.at[right, b], w_all.at[right, b], {"zh": h_down}))
        w_in.append(send(w_all.at[left], w_all.at[left], sib))
        w_in.append(send(w_all.at[right], w_all.at[right], sib))

    def w_share():
        far = h_far * NC + c
        w_in[3].wait_recv()
        w_in.append(send(w_all.at[far, pl.ds(0, 32)], w_all.at[far, pl.ds(0, 32)], sib))
        w_in[4].wait_recv()
        w_in.append(send(w_all.at[far, pl.ds(32, 32)], w_all.at[far, pl.ds(32, 32)], sib))

    others = pl.ds(1, NY - 1)
    tok_x = []

    def tok_spread():
        for copy in tok_in:
            copy.wait_recv()
        quarter = tok.at[others, x]
        tok_x.append(send(quarter, quarter, {"x": x_up}))
        tok_x.append(send(quarter, quarter, {"x": x_down}))

    def tok_forward():
        tok_x[0].wait_recv()
        tok_x[1].wait_recv()
        a = tok.at[others, x_down, pl.ds(0, 16)]
        b = tok.at[others, x_up, pl.ds(16, 16)]
        tok_x.append(send(a, a, {"x": x_up}))
        tok_x.append(send(b, b, {"x": x_down}))

    def tok_turn():
        tok_x[2].wait_recv()
        tok_x[3].wait_recv()
        for j in range(NY):
            if j == 0:
                block = tokens[:, pl.ds(pl.multiple_of(y * 512, 512), 512)]
            else:
                block = tok[j].reshape(128, 512)
            turned = block.T
            for h in range(NH):
                for core in range(NC):
                    row = (h * NC + core) * 64
                    tok_t[core, h * 64 : h * 64 + 64, j * 128 : j * 128 + 128] = turned[row : row + 64]

    share = {}
    rs = {}

    def grad_part(k, core):
        ups = up[k][...].reshape(NY * 128, chunks[k][1])
        part = jnp.dot(tok_t[core], ups, preferred_element_type=F32)
        return part.reshape(NH, 64, chunks[k][1])

    def grad_other(k):
        b_send[k][...] = grad_part(k, 1 - c).astype(BF16)
        share[k] = send(b_send[k], b_recv[k], sib)

    def grad_own(k):
        b_own[k][...] = grad_part(k, c)

    def z1(k):
        share[k].wait_recv()
        total = b_own[k][...] + b_recv[k][...].astype(F32)
        b_own[k][...] = total
        b_sum[k][...] = total.astype(BF16)
        rs[k] = [
            send(b_sum[k].at[h_far, pl.ds(0, 32)], b_a[k], {"zh": h_up}),
            send(b_sum[k].at[h_far, pl.ds(32, 32)], b_b[k], {"zh": h_down}),
        ]

    def z2(k):
        rs[k][0].wait_recv()
        b_tp[k][0:32] = (b_own[k][h_up, 0:32] + b_a[k][...].astype(F32)).astype(BF16)
        b_tp[k][32:64] = b_own[k][h_up, 32:64].astype(BF16)
        rs[k].append(send(b_tp[k], b_l[k], {"zh": h_up}))
        rs[k][1].wait_recv()
        b_tm[k][0:32] = b_own[k][h_down, 0:32].astype(BF16)
        b_tm[k][32:64] = (b_own[k][h_down, 32:64] + b_b[k][...].astype(F32)).astype(BF16)
        rs[k].append(send(b_tm[k], b_r[k], {"zh": h_down}))

    def z3(k):
        rs[k][2].wait_recv()
        rs[k][3].wait_recv()
        total = b_own[k][zh] + b_l[k][...].astype(F32) + b_r[k][...].astype(F32)
        at, width = chunks[k]
        wg_out[:, at : at + width] = accum[:, at : at + width] + total * norm

    px = {}

    def partial(g):
        first, n = GROUPS[g][0], len(GROUPS[g])
        total = None
        for k, (at, width) in enumerate(chunks):
            lhs = up[k][first : first + n].reshape(n * 128, width)
            rhs = w_all[:, :, at : at + width].reshape(NH * NC * 64, width)
            term = lax.dot_general(
                lhs, rhs, (((1,), (1,)), ((), ())), preferred_element_type=F32
            )
            total = term if total is None else total + term
        p_all[g][...] = total.astype(BF16).reshape(n, NX, 32, 512)
        px[g] = [
            send(p_all[g].at[:, x_far, pl.ds(0, 16)], p_a[g], {"x": x_up}),
            send(p_all[g].at[:, x_far, pl.ds(16, 16)], p_b[g], {"x": x_down}),
        ]

    def x2(g):
        px[g][0].wait_recv()
        p_tp[g][:, 0:16] = (p_all[g][:, x_up, 0:16].astype(F32) + p_a[g][...].astype(F32)).astype(BF16)
        p_tp[g][:, 16:32] = p_all[g][:, x_up, 16:32]
        px[g].append(send(p_tp[g], p_l[g], {"x": x_up}))
        px[g][1].wait_recv()
        p_tm[g][:, 0:16] = p_all[g][:, x_down, 0:16]
        p_tm[g][:, 16:32] = (
            p_all[g][:, x_down, 16:32].astype(F32) + p_b[g][...].astype(F32)
        ).astype(BF16)
        px[g].append(send(p_tm[g], p_r[g], {"x": x_down}))

    def x3(g):
        px[g][2].wait_recv()
        px[g][3].wait_recv()
        total = p_all[g][:, x].astype(F32) + p_l[g][...].astype(F32) + p_r[g][...].astype(F32)
        n = len(GROUPS[g])
        total = total.reshape(n, NL, 16, 512)
        p_sum[g][...] = total
        p_half[g][...] = total.astype(BF16)
        px[g].append(send(p_half[g].at[:, 1 - zl], p_z[g], pair))

    def x4(g):
        px[g][4].wait_recv()
        p_fin[g][...] = (p_sum[g][:, zl] + p_z[g][...].astype(F32)).astype(BF16)
        for i, j in enumerate(GROUPS[g]):
            if j == 0:

                @pl.when(t == y)
                def _():
                    fin[x, zl] = p_fin[g][i]

                @pl.when(t != y)
                def _():
                    fin_copy(j, p_fin[g].at[i], t).start()

            else:
                fin_copy(j, p_fin[g].at[i], t).start()

    arrived(0, 1); pass_on(0, 1)
    arrived(1, 1); pass_on(1, 1)
    w_forward()
    arrived(0, 2); pass_on(0, 2); pass_on(2, 0)
    tok_spread()
    arrived(0, 3); pass_on(0, 3)
    w_share()
    arrived(1, 2); pass_on(1, 2)
    tok_forward()
    arrived(2, 1); pass_on(2, 1)
    arrived(0, 4)
    tok_turn()
    grad_other(0); grad_own(0)
    arrived(1, 3); pass_on(1, 3); pass_on(3, 0)
    arrived(2, 2); pass_on(2, 2)
    z1(0)
    arrived(3, 1); pass_on(3, 1)
    arrived(1, 4)
    grad_other(1); grad_own(1)
    z2(0)
    arrived(2, 3); pass_on(2, 3)
    z1(1)
    z3(0)
    w_in[2].wait_recv()
    for copy in w_in[5:]:
        copy.wait_recv()
    arrived(3, 2); pass_on(3, 2)
    partial(0)
    z2(1)
    arrived(2, 4)
    grad_other(2); grad_own(2)
    arrived(3, 3); pass_on(3, 3)
    partial(1)
    x2(0)
    z1(2)
    partial(2)
    x2(1)
    x3(0)
    z3(1)
    arrived(3, 4)
    grad_other(3)
    partial(3)
    grad_own(3)
    z2(2)
    x2(2)
    x3(1)
    x4(0)
    z1(3)
    x2(3)
    x3(2)
    x4(1)
    z2(3)
    x3(3)
    x4(2)
    z3(2)
    x4(3)
    z3(3)

    for other in range(NX * NL):

        @pl.when(jnp.logical_or(t != y, t != other))
        def _():
            fin_copy(0, p_fin[0].at[0], other).wait_recv()

    ig_out[...] = fin[...].reshape(128, 512)
    for copy in copies:
        copy.wait_send()
    assert len(copies) == n_copies

    @pl.when(t != y)
    def _():
        fin_copy(0, p_fin[0].at[0], t).wait_send()

    for g, group in enumerate(GROUPS):
        for i, j in enumerate(group):
            if j:
                fin_copy(j, p_fin[g].at[i], t).wait_send()


def on_device(tokens, gate_pre, hid_grad, up_weight, grad_accum):
    rows, channels = tokens.shape
    w_rows, width = up_weight.shape
    norm = 1.0 / math.sqrt(rows * NY * NH * NC)
    chunks = chunks_of(width)
    n_copies = 8 * len(chunks) + 7 + 4 + 9 + 5 * len(chunks) + 5 * len(GROUPS)
    dma, vmem = pltpu.SemaphoreType.DMA, pltpu.VMEM
    widths = [w for _, w in chunks]
    sizes = [len(g) for g in GROUPS]
    scratch = [dma((n_copies,)), dma((n_copies,)), dma((NY,)), dma((NX * NL,))]
    scratch += [
        vmem((NY, NX, 32, 512), BF16),
        vmem((NC, 256, 1024), BF16),
        vmem((NH * NC, w_rows, width), BF16),
        vmem((NX, NL, 16, 512), BF16),
    ]
    scratch += [vmem((NY, rows, w), BF16) for w in widths]
    for shape, kind in (
        ((NH, 64), BF16), ((NH, 64), BF16), ((NH, 64), F32), ((NH, 64), BF16),
        ((32,), BF16), ((32,), BF16), ((64,), BF16), ((64,), BF16), ((64,), BF16), ((64,), BF16),
    ):
        scratch += [vmem((*shape, w), kind) for w in widths]
    for shape, kind in (
        ((NX, 32, 512), BF16), ((16, 512), BF16), ((16, 512), BF16), ((32, 512), BF16),
        ((32, 512), BF16), ((32, 512), BF16), ((32, 512), BF16),
        ((NL, 16, 512), F32), ((NL, 16, 512), BF16), ((16, 512), BF16), ((16, 512), BF16),
    ):
        scratch += [vmem((n, *shape), kind) for n in sizes]
    return pl.pallas_call(
        functools.partial(kernel, norm, chunks, n_copies),
        out_shape=(
            jax.ShapeDtypeStruct((w_rows, width), F32),
            jax.ShapeDtypeStruct((rows, channels // NY), BF16),
        ),
        in_specs=[pl.BlockSpec(memory_space=pltpu.VMEM)] * 5,
        out_specs=(pl.BlockSpec(memory_space=pltpu.VMEM),) * 2,
        scratch_shapes=scratch,
        compiler_params=pltpu.CompilerParams(
            collective_id=0, has_side_effects=True, vmem_limit_bytes=48 * 1024 * 1024
        ),
    )(tokens, gate_pre, hid_grad, up_weight, grad_accum)


def solution(mesh):
    fine = Mesh(mesh.devices.reshape(NY, NH, NC, NX, NL), ("y", "zh", "c", "x", "zl"))
    fsdp = ("y", "zh", "c")
    rows, both = P(fsdp, None), P(fsdp, ("x", "zl"))
    return jax.shard_map(
        on_device,
        mesh=fine,
        in_specs=(rows, both, both, both, both),
        out_specs=(both, both),
        check_vma=False,
    )
```

time: 225 us -> 92.6 us (0.41)
  the two profiles are of different devices: /device:TPU:1 before, /device:TPU:4 now
where the time goes in v2:
time: 92.6 us; the launch traced here: 92.5 us
  Pallas kernels  87.6 us (95%)
  local copies, waits for them, and re-layouts  4.15 us (4%)
    pallas_call x1, Pallas kernels, on_device(): pl.pallas_call(functools.partial(kernel, norm, chunks, n_copies), out_sha...  87.6 us
    unnamed x10, local copies, waits for them, and re-layouts  4.15 us

profile of v2, /device:TPU:4, one launch (start us, length us, event | category | flops | bytes accessed | tf_op | source)
XLA Modules:
  0.0 92.5 jit_solution(6842261980271169616)
XLA Ops:
  0.6 0.0 copy-start
  0.6 1.4 %copy.7.gate = bf16[128,1848]{1,0:T(8,128)(2,1)S(1)} copy(bf16[128,1848]{0,1:T(8,128)(2,1)} %param.6) | data formatting | bytes 946176 | tf_op args[1]
  2.0 0.0 copy-start.1
  2.0 0.0 copy-start.2
  2.0 1.3 %copy.8.hid = bf16[128,1848]{1,0:T(8,128)(2,1)S(1)} copy(bf16[128,1848]{0,1:T(8,128)(2,1)} %param.7) | data formatting | bytes 946176 | tf_op args[2]
  3.4 0.0 copy-done
  3.4 0.0 copy-done.1
  3.4 0.0 copy-done.2
  3.4 87.6 %shard_map.68 = (f32[64,1848]{1,0:T(8,128)S(1)}, bf16[128,512]{1,0:T(8,128)(2,1)S(1)}) custom-call(bf16[128,4096]{1,0:T(8,128)(2,1)S(1)} %copy-done, bf16[128,1848]{1,0:T(8,128)(2,1)S(1)} %copy.7.gate, bf16[128,1848]{1,0:T(8,128)(2,1)S(1)} %copy.8.hid, bf16[64,1848]{1,0:T(8,128)(2,1)S(1)} %copy-done.2, f32[64,1848]{1,0:T(8,128)S(1)} %copy-done.1), custom_call_target="tpu_custom_call" | custom-call | tf_op jit(solution)/shard_map/pallas_call | solution.py:390
  91.0 0.8 copy.11
  91.8 0.7 copy.12
Async XLA Ops:
  0.6 2.7 %copy-start = (bf16[128,4096]{1,0:T(8,128)(2,1)S(1)}, bf16[128,4096]{1,0:T(8,128)(2,1)}, u32[]{:S(2)}) copy-start(bf16[128,4096]{1,0:T(8,128)(2,1)} %tokens.1) | copy-start | bytes 3145732
  2.0 1.4 %copy-start.1 = (f32[64,1848]{1,0:T(8,128)S(1)}, f32[64,1848]{1,0:T(8,128)}, u32[]{:S(2)}) copy-start(f32[64,1848]{1,0:T(8,128)} %accum.1) | copy-start | bytes 1419268
  2.0 1.4 %copy-start.2 = (bf16[64,1848]{1,0:T(8,128)(2,1)S(1)}, bf16[64,1848]{1,0:T(8,128)(2,1)}, u32[]{:S(2)}) copy-start(bf16[64,1848]{1,0:T(8,128)(2,1)} %w_own.1) | copy-start | bytes 709636

commit v3 on v1

v3 whole, which is shorter than its diff:
```python
import functools
import math

import jax
import jax.numpy as jnp
from jax import lax
from jax.experimental import pallas as pl
from jax.experimental.pallas import tpu as pltpu
from jax.sharding import Mesh, PartitionSpec as P

NY, NH, NC, NX, NL = 8, 4, 2, 4, 2
OFF = (0, 1, -1, 2, -2, 3, -3, 4)
BACK = (0, 2, 1, 4, 3, 6, 5, 7)
PLUS, MINUS = (0, 2, 4, 6, 7), (0, 1, 3, 5, 7)
TEAMS = ((0,), (1, 2), (3, 4), (5, 6), (7,))
SPLIT = (640, 1152, 1536)
F32, BF16 = jnp.float32, jnp.bfloat16
PLAN = (
    ("up", 0), ("enter",), ("ring", 0, 0, 0), ("w_send",), ("up", 1), ("ring", 1, 0, 0), ("up", 2),
    ("tok_send",), ("ring", 1, 1, 0), ("ring", 0, 1, 0), ("ring", 0, 0, 1), ("tok_pair",),
    ("ring", 1, 1, 1), ("ring", 1, 0, 1), ("up", 3), ("ring", 0, 1, 1), ("ring", 0, 0, 2),
    ("w_forward",), ("tok_spread",), ("ring", 1, 0, 2), ("ring", 0, 1, 2), ("ring", 2, 1, 0),
    ("ring", 0, 0, 3), ("ring", 2, 0, 0), ("tok_forward",), ("ring", 0, 1, 3), ("ring", 1, 1, 2),
    ("w_share",), ("ring", 3, 0, 0), ("ring", 2, 1, 1), ("ring", 3, 1, 0), ("w_ready",),
    ("p_begin", 0), ("ring", 2, 0, 1), ("got", 0, 0, 4), ("ring", 1, 0, 3), ("p_begin", 1),
    ("got", 0, 1, 4), ("tok_turn",), ("grad_other", 0), ("p_send", 0), ("ring", 1, 1, 3),
    ("ring", 3, 0, 1), ("grad_own", 0), ("ring", 2, 1, 2), ("z_send", 0), ("ring", 3, 1, 1),
    ("p_send", 1), ("ring", 2, 0, 2), ("p_begin", 2), ("got", 1, 0, 4), ("ring", 3, 0, 2),
    ("got", 1, 1, 4), ("grad_other", 1), ("grad_own", 1), ("ring", 2, 1, 3), ("ring", 3, 1, 2),
    ("p_send", 2), ("ring", 2, 0, 3), ("z_send", 1), ("ring", 3, 0, 3), ("p_begin", 3),
    ("ring", 3, 1, 3), ("got", 2, 1, 4), ("p_send", 3), ("got", 2, 0, 4), ("grad_other", 2),
    ("grad_own", 2), ("p_end", 0), ("p_begin", 4), ("got", 3, 0, 4), ("p_end", 1), ("got", 3, 1, 4),
    ("z_send", 2), ("z_end", 0), ("p_end", 2), ("p_send", 4), ("grad_other", 3), ("grad_own", 3),
    ("p_end", 3), ("z_send", 3), ("p_end", 4), ("drain",), ("z_end", 1), ("z_end", 2), ("z_end", 3),
)


def kernel(norm, chunks, n_copies, tokens, gate_in, hid_in, w_own, accum_in, wg_out, ig_out, *scratch):
    scratch = list(scratch)
    take = lambda n: [scratch.pop(0) for _ in range(n)]
    nk = len(chunks)
    send_sem, recv_sem, fin_send, fin_recv, load_sem = take(5)
    gate, hid, accum, wg, ig, tok_own, tok, tok_t, w_all, fin = take(10)
    up = take(nk)
    b_send, b_recv, b_own, b_sum, b_l, b_r, b_f = (take(nk) for _ in range(7))
    nt = len(TEAMS)
    p_acc, p_all, p_l, p_r, p_f, p_fin = (take(nt) for _ in range(6))

    y, zh, c, x, zl = (lax.axis_index(a) for a in ("y", "zh", "c", "x", "zl"))
    zc, t = zh * NC + c, x * NL + zl
    around = lambda v, n: lax.rem(v + n, n)
    y_up, y_down = {"y": around(y + 1, NY)}, {"y": around(y - 1, NY)}
    h_up, h_down = around(zh + 1, NH), around(zh - 1, NH)
    h_far = around(zh + 2, NH)
    x_up, x_down, x_far = around(x + 1, NX), around(x - 1, NX), around(x + 2, NX)
    sib = {"c": 1 - c}
    fin_x, fin_l = y // NL, lax.rem(y, NL)
    MESH = pl.DeviceIdType.MESH

    copies = []

    def send(src, dst, device):
        i = len(copies)
        copy = pltpu.make_async_remote_copy(
            src_ref=src,
            dst_ref=dst,
            send_sem=send_sem.at[i],
            recv_sem=recv_sem.at[i],
            device_id=device,
            device_id_type=MESH,
        )
        copy.start()
        copies.append(copy)
        return copy

    def fin_copy(j, src, sem):
        return pltpu.make_async_remote_copy(
            src_ref=src,
            dst_ref=fin.at[x, zl],
            send_sem=fin_send.at[j],
            recv_sem=fin_recv.at[sem],
            device_id={"y": around(y + OFF[j], NY), "x": fin_x, "zl": fin_l},
            device_id_type=MESH,
        )

    barrier = pltpu.get_barrier_semaphore()

    def greet(device):
        pl.semaphore_signal(barrier, inc=1, device_id=device, device_id_type=MESH)

    for j in range(1, NY):
        greet({"y": around(y + OFF[j], NY)})
    for h in (h_up, h_down, h_far):
        greet({"zh": h})
    for v in (x_up, x_down, x_far):
        greet({"x": v})
    greet({"zl": 1 - zl})
    greet(sib)
    for other in range(NX * NL):

        @pl.when(jnp.logical_or(t != y, t != other))
        def _():
            greet({"y": t, "x": other // NL, "zl": other % NL})

    loads = {}

    def load(name, src, dst):
        loads[name] = pltpu.make_async_copy(src, dst, load_sem.at[len(loads)])
        loads[name].start()

    for k, (at, width) in enumerate(chunks):
        part = pl.ds(at, width)
        load((0, k), gate_in.at[part], gate.at[part])
        load((1, k), hid_in.at[part], hid.at[part])

    def load_rest():
        load("w", w_own, w_all.at[zc])
        columns = pl.ds(pl.multiple_of(y * 512, 512), 512)
        load("tok", tokens.at[:, columns], tok_own)
        load("accum", accum_in, accum)

    def up_grad(k):
        loads[0, k].wait()
        loads[1, k].wait()
        at, width = chunks[k]
        v = gate[at : at + width].astype(F32)
        g = hid[at : at + width].astype(F32)
        up[k][0] = (g * (v / (1.0 + jnp.exp(-v)))).astype(BF16).T

    ring = {}

    def arrived(k, half, s):
        for way in (0, 1):
            if s < 4 or way == half:
                ring[k, half, s - 1, way].wait_recv()

    def ring_step(k, half, s):
        if s:
            arrived(k, half, s)
        rows = pl.ds(half * 64, 64)
        for way, path, device in ((0, PLUS, y_up), (1, MINUS, y_down)):
            if s < 3 or way == half:
                ring[k, half, s, way] = send(
                    up[k].at[path[s], rows], up[k].at[path[s + 1], rows], device
                )

    tok_in, tok_x = [], []
    others = pl.ds(1, NY - 1)

    def tok_send():
        for j in range(1, NY):
            to = around(y + OFF[j], NY)
            rows = pl.ds(pl.multiple_of(t * 16, 16), 16)
            columns = pl.ds(pl.multiple_of(to * 512, 512), 512)
            tok_in.append(send(tokens.at[rows, columns], tok.at[BACK[j], x, zl], {"y": to}))

    def tok_pair():
        for copy in tok_in:
            copy.wait_recv()
        eighth = tok.at[others, x, zl]
        tok_in.append(send(eighth, eighth, {"zl": 1 - zl}))

    def tok_spread():
        tok_in[NY - 1].wait_recv()
        quarter = tok.at[others, x]
        tok_x.append(send(quarter, quarter, {"x": x_up}))
        tok_x.append(send(quarter, quarter, {"x": x_down}))

    def tok_forward():
        tok_x[0].wait_recv()
        tok_x[1].wait_recv()
        a = tok.at[others, x_down, 0]
        b = tok.at[others, x_up, 1]
        tok_x.append(send(a, a, {"x": x_up}))
        tok_x.append(send(b, b, {"x": x_down}))

    def tok_turn():
        tok_x[2].wait_recv()
        tok_x[3].wait_recv()
        for j in range(NY):
            if j == 0:
                loads["tok"].wait()
                block = tok_own[...]
            else:
                block = tok[j].reshape(128, 512)
            turned = block.T
            for h in range(NH):
                for core in range(NC):
                    row = (h * NC + core) * 64
                    tok_t[core, h * 64 : h * 64 + 64, j * 128 : j * 128 + 128] = turned[row : row + 64]

    w_in = []

    def w_send():
        for device in ({"zh": h_up}, {"zh": h_down}, sib):
            w_in.append(send(w_own, w_all.at[zc], device))
        load_rest()

    def w_forward():
        w_in[0].wait_recv()
        w_in[1].wait_recv()
        left, right = h_down * NC + c, h_up * NC + c
        a, b = pl.ds(0, 32), pl.ds(32, 32)
        w_in.append(send(w_all.at[left, a], w_all.at[left, a], {"zh": h_up}))
        w_in.append(send(w_all.at[right, b], w_all.at[right, b], {"zh": h_down}))
        w_in.append(send(w_all.at[left], w_all.at[left], sib))
        w_in.append(send(w_all.at[right], w_all.at[right], sib))

    def w_share():
        far = h_far * NC + c
        w_in[3].wait_recv()
        w_in.append(send(w_all.at[far, pl.ds(0, 32)], w_all.at[far, pl.ds(0, 32)], sib))
        w_in[4].wait_recv()
        w_in.append(send(w_all.at[far, pl.ds(32, 32)], w_all.at[far, pl.ds(32, 32)], sib))

    def w_ready():
        loads["w"].wait()
        w_in[2].wait_recv()
        for copy in w_in[5:]:
            copy.wait_recv()

    share, zs = {}, {}

    def grad_part(k, core):
        ups = up[k][...].reshape(NY * 128, chunks[k][1])
        part = jnp.dot(tok_t[core], ups, preferred_element_type=F32)
        return part.reshape(NH, 64, chunks[k][1])

    def grad_other(k):
        b_send[k][...] = grad_part(k, 1 - c).astype(BF16)
        share[k] = send(b_send[k], b_recv[k], sib)

    def grad_own(k):
        b_own[k][...] = grad_part(k, c)

    def z_send(k):
        share[k].wait_recv()
        total = b_own[k][...] + b_recv[k][...].astype(F32)
        b_own[k][...] = total
        b_sum[k][...] = total.astype(BF16)
        zs[k] = [
            send(b_sum[k].at[h], into[k], {"zh": h})
            for h, into in ((h_far, b_f), (h_up, b_l), (h_down, b_r))
        ]

    def z_end(k):
        for copy in zs[k]:
            copy.wait_recv()
        if k == 0:
            loads["accum"].wait()
        total = b_own[k][zh]
        for other in (b_l, b_r, b_f):
            total = total + other[k][...].astype(F32)
        at, width = chunks[k]
        wg[:, at : at + width] = accum[:, at : at + width] + total * norm
        load((2, k), wg.at[:, pl.ds(at, width)], wg_out.at[:, pl.ds(at, width)])

    xs = {}

    def term(p, ks):
        first, n = TEAMS[p][0], len(TEAMS[p])
        total = None
        for k, cut in [(k, cut) for k in ks for cut in range(0, chunks[k][1], 512)]:
            at, width = chunks[k]
            end = min(cut + 512, width)
            lhs = up[k][first : first + n, :, cut:end].reshape(n * 128, end - cut)
            rhs = w_all[:, :, at + cut : at + end].reshape(NH * NC * 64, end - cut)
            one = lax.dot_general(lhs, rhs, (((1,), (1,)), ((), ())), preferred_element_type=F32)
            total = one if total is None else total + one
        return total

    def p_begin(p):
        p_acc[p][...] = term(p, range(nk - 1))

    def p_send(p):
        total = p_acc[p][...] + term(p, (nk - 1,))
        p_all[p][...] = total.astype(BF16).reshape(len(TEAMS[p]), NX, 32, 512)
        xs[p] = [
            send(p_all[p].at[:, v], into[p], {"x": v})
            for v, into in ((x_far, p_f), (x_up, p_l), (x_down, p_r))
        ]

    def p_end(p):
        for copy in xs[p]:
            copy.wait_recv()
        total = p_all[p][:, x].astype(F32)
        for other in (p_l, p_r, p_f):
            total = total + other[p][...].astype(F32)
        p_fin[p][...] = total.astype(BF16)
        for i, j in enumerate(TEAMS[p]):
            if j == 0:

                @pl.when(t == y)
                def _():
                    fin[x, zl] = p_fin[p][i]

                @pl.when(t != y)
                def _():
                    fin_copy(j, p_fin[p].at[i], t).start()

            else:
                fin_copy(j, p_fin[p].at[i], t).start()

    drained = []

    def drain():
        for copy in copies[len(drained) :]:
            copy.wait_send()
            drained.append(copy)

    def enter():
        pl.semaphore_wait(barrier, NY - 1 + 8 + jnp.where(t == y, NX * NL - 1, NX * NL))

    steps = {
        "enter": enter, "drain": drain, "up": up_grad, "ring": ring_step, "got": arrived,
        "tok_send": tok_send, "tok_pair": tok_pair, "tok_spread": tok_spread, "tok_forward": tok_forward, "tok_turn": tok_turn,
        "w_send": w_send, "w_forward": w_forward, "w_share": w_share, "w_ready": w_ready,
        "grad_other": grad_other, "grad_own": grad_own, "z_send": z_send, "z_end": z_end,
        "p_begin": p_begin, "p_send": p_send, "p_end": p_end,
    }
    for step, *of in PLAN:
        steps[step](*of)

    for other in range(NX * NL):

        @pl.when(jnp.logical_or(t != y, t != other))
        def _():
            fin_copy(0, p_fin[0].at[0], other).wait_recv()

    ig[...] = (fin[:, 0].astype(F32) + fin[:, 1].astype(F32)).astype(BF16).reshape(128, 512)
    load("ig", ig, ig_out)
    drain()
    loads["ig"].wait()
    for k in range(nk):
        loads[2, k].wait()
    assert len(copies) == n_copies

    @pl.when(t != y)
    def _():
        fin_copy(0, p_fin[0].at[0], t).wait_send()

    for p, team in enumerate(TEAMS):
        for i, j in enumerate(team):
            if j:
                fin_copy(j, p_fin[p].at[i], t).wait_send()


def on_device(tokens, gate_pre, hid_grad, up_weight, grad_accum):
    rows, channels = tokens.shape
    w_rows, width = up_weight.shape
    norm = 1.0 / math.sqrt(rows * NY * NH * NC)
    ends = (*SPLIT, width)
    chunks = [(at, end - at) for at, end in zip((0, *SPLIT), ends)]
    n_copies = 14 * len(chunks) + 8 + 4 + 9 + 4 * len(chunks) + 3 * len(TEAMS)
    dma, vmem = pltpu.SemaphoreType.DMA, pltpu.VMEM
    widths = [w for _, w in chunks]
    sizes = [len(team) for team in TEAMS]
    scratch = [dma((n_copies,)), dma((n_copies,)), dma((NY,)), dma((NX * NL,))]
    scratch += [dma((3 * len(chunks) + 4,))]
    scratch += [
        vmem((width, rows), BF16),
        vmem((width, rows), BF16),
        vmem((w_rows, width), F32),
        vmem((w_rows, width), F32),
        vmem((rows, 512), BF16),
        vmem((rows, 512), BF16),
        vmem((NY, NX, NL, 16, 512), BF16),
        vmem((NC, 256, 1024), BF16),
        vmem((NH * NC, w_rows, width), BF16),
        vmem((NX, NL, 32, 512), BF16),
    ]
    scratch += [vmem((NY, rows, w), BF16) for w in widths]
    for shape, kind in (
        ((NH, 64), BF16), ((NH, 64), BF16), ((NH, 64), F32), ((NH, 64), BF16),
        ((64,), BF16), ((64,), BF16), ((64,), BF16),
    ):
        scratch += [vmem((*shape, w), kind) for w in widths]
    scratch += [vmem((n * 128, 512), F32) for n in sizes]
    scratch += [vmem((n, NX, 32, 512), BF16) for n in sizes]
    for _ in range(4):
        scratch += [vmem((n, 32, 512), BF16) for n in sizes]
    return pl.pallas_call(
        functools.partial(kernel, norm, chunks, n_copies),
        out_shape=(
            jax.ShapeDtypeStruct((w_rows, width), F32),
            jax.ShapeDtypeStruct((rows, channels // NY), BF16),
        ),
        in_specs=[pl.BlockSpec(memory_space=pltpu.HBM)] * 5,
        out_specs=(pl.BlockSpec(memory_space=pltpu.HBM),) * 2,
        scratch_shapes=scratch,
        compiler_params=pltpu.CompilerParams(
            collective_id=0, has_side_effects=True, vmem_limit_bytes=56 * 1024 * 1024
        ),
    )(tokens, gate_pre.T, hid_grad.T, up_weight, grad_accum)


def solution(mesh):
    fine = Mesh(mesh.devices.reshape(NY, NH, NC, NX, NL), ("y", "zh", "c", "x", "zl"))
    fsdp = ("y", "zh", "c")
    rows, both = P(fsdp, None), P(fsdp, ("x", "zl"))
    return jax.shard_map(
        on_device,
        mesh=fine,
        in_specs=(rows, both, both, both, both),
        out_specs=(both, both),
        check_vma=False,
    )
```

time: 225 us -> 80.1 us (0.36)
  waiting for transfers between devices: 180 us -> 0 us
  Pallas kernels: 0 us -> 76.8 us
  between operations: 13.8 us -> 0.65 us
  matrix products: 10.3 us -> 0 us
  starting transfers between devices: 9.36 us -> 0 us
  local copies, waits for them, and re-layouts: 8.57 us -> 2.53 us
  other arithmetic: 2.34 us -> 0 us
    all_gather x2 -> x0, waiting for transfers between devices: 93.3 us -> none  [the longest x1 59.1 us: on_device(): ups = lax.all_gather(up_grad, 'y', axis=0, tiled=True)]
    pallas_call x0 -> x1, Pallas kernels: none -> 76.8 us  [on_device(): pl.pallas_call(functools.partial(kernel, norm, chunks, n_copies), out_sha...]
    unnamed x5 -> x0, waiting for transfers between devices: 49.4 us -> none
    reduce_scatter x1 -> x0, waiting for transfers between devices: 36.8 us -> none  [on_device(): lax.psum_scatter(partial_value, 'tp', scatter_dimension=0, tiled=True)]
    dot_general x2 -> x0, matrix products: 10.3 us -> none  [the longest x1 6.09 us: on_device(): lax.dot_general(ups, weight, (((1,), (1,)), ((), ())), preferred_element_...]
    all_to_all x1 -> x0, starting transfers between devices: 7.65 us -> none  [on_device(): lax.all_to_all(tokens.reshape(rows, n_y, block), 'y', 1, 0, tiled=True)]
    unnamed x8 -> x4, local copies, waits for them, and re-layouts: 8.04 us -> 2.53 us
  transfers between devices with their start and end apart: 6 -> 0, of which waited for: 4 -> 0; matrix products, arithmetic and copies ran while one was open for 8% -> 0% of each run, Pallas kernels for 0% -> 0%
where the time goes in v3:
time: 80.1 us; the launch traced here: 80 us
  Pallas kernels  76.8 us (96%)
  local copies, waits for them, and re-layouts  2.53 us (3%)
    pallas_call x1, Pallas kernels, on_device(): pl.pallas_call(functools.partial(kernel, norm, chunks, n_copies), out_sha...  76.8 us
    unnamed x4, local copies, waits for them, and re-layouts  2.53 us

profile of v3, /device:TPU:1, one launch (start us, length us, event | category | flops | bytes accessed | tf_op | source)
XLA Modules:
  0.0 80.0 jit_solution(13950382727075804955)
XLA Ops:
  0.6 76.8 %shard_map.68 = (f32[64,1848]{1,0:T(8,128)}, bf16[128,512]{1,0:T(8,128)(2,1)}) custom-call(bf16[128,4096]{1,0:T(8,128)(2,1)} %tokens.1, bf16[1848,128]{1,0:T(8,128)(2,1)} %bitcast.2, bf16[1848,128]{1,0:T(8,128)(2,1)} %bitcast.3, bf16[64,1848]{1,0:T(8,128)(2,1)} %w_own.1, f32[64,1848]{1,0:T(8,128)} %accum_in.1), custom_call_target="tpu_custom_call" | custom-call | tf_op jit(solution)/shard_map/pallas_call | solution.py:382
  77.4 0.0 copy-start
  77.4 1.9 %copy.9 = f32[64,1848]{1,0:T(8,128)} copy(f32[64,1848]{1,0:T(8,128)} %get-tuple-element.4) | data formatting | bytes 946176
  79.3 0.0 copy-done
  79.3 0.7 copy.10
Async XLA Ops:
  77.4 1.9 %copy-start = (bf16[128,512]{1,0:T(8,128)(2,1)S(1)}, bf16[128,512]{1,0:T(8,128)(2,1)}, u32[]{:S(2)}) copy-start(bf16[128,512]{1,0:T(8,128)(2,1)} %get-tuple-element.5) | copy-start | bytes 393220

commit v4 on v3

--- a/solution.py
+++ b/solution.py
@@ -13,36 +13,37 @@
 BACK = (0, 2, 1, 4, 3, 6, 5, 7)
 PLUS, MINUS = (0, 2, 4, 6, 7), (0, 1, 3, 5, 7)
 TEAMS = ((0,), (1, 2), (3, 4), (5, 6), (7,))
-SPLIT = (640, 1152, 1536)
+SPLIT = (512, 1024, 1536)
 F32, BF16 = jnp.float32, jnp.bfloat16
 PLAN = (
-    ("up", 0), ("enter",), ("ring", 0, 0, 0), ("w_send",), ("up", 1), ("ring", 1, 0, 0), ("up", 2),
-    ("tok_send",), ("ring", 1, 1, 0), ("ring", 0, 1, 0), ("ring", 0, 0, 1), ("tok_pair",),
-    ("ring", 1, 1, 1), ("ring", 1, 0, 1), ("up", 3), ("ring", 0, 1, 1), ("ring", 0, 0, 2),
-    ("w_forward",), ("tok_spread",), ("ring", 1, 0, 2), ("ring", 0, 1, 2), ("ring", 2, 1, 0),
-    ("ring", 0, 0, 3), ("ring", 2, 0, 0), ("tok_forward",), ("ring", 0, 1, 3), ("ring", 1, 1, 2),
-    ("w_share",), ("ring", 3, 0, 0), ("ring", 2, 1, 1), ("ring", 3, 1, 0), ("w_ready",),
-    ("p_begin", 0), ("ring", 2, 0, 1), ("got", 0, 0, 4), ("ring", 1, 0, 3), ("p_begin", 1),
-    ("got", 0, 1, 4), ("tok_turn",), ("grad_other", 0), ("p_send", 0), ("ring", 1, 1, 3),
-    ("ring", 3, 0, 1), ("grad_own", 0), ("ring", 2, 1, 2), ("z_send", 0), ("ring", 3, 1, 1),
-    ("p_send", 1), ("ring", 2, 0, 2), ("p_begin", 2), ("got", 1, 0, 4), ("ring", 3, 0, 2),
-    ("got", 1, 1, 4), ("grad_other", 1), ("grad_own", 1), ("ring", 2, 1, 3), ("ring", 3, 1, 2),
-    ("p_send", 2), ("ring", 2, 0, 3), ("z_send", 1), ("ring", 3, 0, 3), ("p_begin", 3),
-    ("ring", 3, 1, 3), ("got", 2, 1, 4), ("p_send", 3), ("got", 2, 0, 4), ("grad_other", 2),
-    ("grad_own", 2), ("p_end", 0), ("p_begin", 4), ("got", 3, 0, 4), ("p_end", 1), ("got", 3, 1, 4),
-    ("z_send", 2), ("z_end", 0), ("p_end", 2), ("p_send", 4), ("grad_other", 3), ("grad_own", 3),
-    ("p_end", 3), ("z_send", 3), ("p_end", 4), ("drain",), ("z_end", 1), ("z_end", 2), ("z_end", 3),
+    ("up", 0), ("enter",), ("ring", 0, 0, 0), ("w_send",), ("ring", 0, 1, 0), ("tok_send",),
+    ("up", 1), ("up", 2), ("ring", 1, 1, 0), ("ring", 0, 1, 1), ("up", 3), ("ring", 2, 1, 0),
+    ("ring", 1, 0, 0), ("tok_pair",), ("ring", 1, 1, 1), ("ring", 0, 0, 1), ("ring", 0, 1, 2),
+    ("w_forward",), ("ring", 1, 0, 1), ("ring", 2, 0, 0), ("tok_spread",), ("ring", 1, 1, 2),
+    ("ring", 0, 0, 2), ("ring", 1, 0, 2), ("ring", 3, 0, 0), ("w_share",), ("ring", 3, 1, 0),
+    ("ring", 0, 1, 3), ("ring", 1, 1, 3), ("tok_forward",), ("ring", 0, 0, 3), ("w_ready",),
+    ("p_begin", 0), ("p_send", 0), ("ring", 1, 0, 3), ("ring", 2, 0, 1), ("ring", 2, 1, 1),
+    ("p_begin", 1), ("ring", 3, 0, 1), ("ring", 3, 1, 1), ("p_send", 1), ("got", 0, 1, 4),
+    ("tok_turn",), ("got", 0, 0, 4), ("grad_other", 0), ("grad_own", 0), ("got", 1, 1, 4),
+    ("got", 1, 0, 4), ("grad_other", 1), ("ring", 2, 0, 2), ("z_send", 0), ("grad_own", 1),
+    ("ring", 2, 1, 2), ("z_send", 1), ("ring", 3, 1, 2), ("ring", 3, 0, 2), ("p_begin", 2),
+    ("p_send", 2), ("ring", 2, 0, 3), ("z_mid", 0), ("ring", 2, 1, 3), ("p_end", 1), ("p_begin", 3),
+    ("ring", 3, 1, 3), ("z_mid", 1), ("ring", 3, 0, 3), ("p_send", 3), ("p_end", 0),
+    ("got", 2, 0, 4), ("got", 2, 1, 4), ("grad_other", 2), ("grad_own", 2), ("p_begin", 4),
+    ("got", 3, 0, 4), ("got", 3, 1, 4), ("grad_other", 3), ("z_send", 2), ("p_send", 4),
+    ("p_end", 2), ("grad_own", 3), ("z_send", 3), ("p_end", 3), ("p_end", 4), ("drain",),
+    ("z_mid", 2), ("z_end", 0), ("z_end", 1), ("z_end", 3), ("z_end", 2),
 )
 
 
-def kernel(norm, chunks, n_copies, tokens, gate_in, hid_in, w_own, accum_in, wg_out, ig_out, *scratch):
+def kernel(chunks, n_copies, tokens, gate_in, hid_in, w_own, wg_out, ig_out, *scratch):
     scratch = list(scratch)
     take = lambda n: [scratch.pop(0) for _ in range(n)]
     nk = len(chunks)
     send_sem, recv_sem, fin_send, fin_recv, load_sem = take(5)
-    gate, hid, accum, wg, ig, tok_own, tok, tok_t, w_all, fin = take(10)
+    gate, hid, tok_own, tok, tok_t, w_all, fin = take(7)
     up = take(nk)
-    b_send, b_recv, b_own, b_sum, b_l, b_r, b_f = (take(nk) for _ in range(7))
+    b_send, b_recv, b_own, b_sum, b_l, b_r, b_f, b_up, b_down = (take(nk) for _ in range(9))
     nt = len(TEAMS)
     p_acc, p_all, p_l, p_r, p_f, p_fin = (take(nt) for _ in range(6))
 
@@ -83,6 +84,19 @@
             device_id_type=MESH,
         )
 
+    loads = {}
+
+    def load(name, src, dst):
+        loads[name] = pltpu.make_async_copy(src, dst, load_sem.at[len(loads)])
+        loads[name].start()
+
+    def load_group(k):
+        part = pl.ds(*chunks[k])
+        load((0, k), gate_in.at[part], gate.at[part])
+        load((1, k), hid_in.at[part], hid.at[part])
+
+    load_group(0)
+
     barrier = pltpu.get_barrier_semaphore()
 
     def greet(device):
@@ -102,22 +116,13 @@
         def _():
             greet({"y": t, "x": other // NL, "zl": other % NL})
 
-    loads = {}
-
-    def load(name, src, dst):
-        loads[name] = pltpu.make_async_copy(src, dst, load_sem.at[len(loads)])
-        loads[name].start()
-
-    for k, (at, width) in enumerate(chunks):
-        part = pl.ds(at, width)
-        load((0, k), gate_in.at[part], gate.at[part])
-        load((1, k), hid_in.at[part], hid.at[part])
+    for k in range(1, nk):
+        load_group(k)
 
     def load_rest():
         load("w", w_own, w_all.at[zc])
         columns = pl.ds(pl.multiple_of(y * 512, 512), 512)
         load("tok", tokens.at[:, columns], tok_own)
-        load("accum", accum_in, accum)
 
     def up_grad(k):
         loads[0, k].wait()
@@ -238,22 +243,36 @@
         total = b_own[k][...] + b_recv[k][...].astype(F32)
         b_own[k][...] = total
         b_sum[k][...] = total.astype(BF16)
-        zs[k] = [
-            send(b_sum[k].at[h], into[k], {"zh": h})
-            for h, into in ((h_far, b_f), (h_up, b_l), (h_down, b_r))
-        ]
+        if k == nk - 1:
+            zs[k] = [
+                send(b_sum[k].at[h], into[k], {"zh": h})
+                for h, into in ((h_far, b_f), (h_up, b_l), (h_down, b_r))
+            ]
+        else:
+            a, b = pl.ds(0, 32), pl.ds(32, 32)
+            zs[k] = [
+                send(b_sum[k].at[h_far, a], b_f[k].at[a], {"zh": h_up}),
+                send(b_sum[k].at[h_far, b], b_f[k].at[b], {"zh": h_down}),
+            ]
+
+    def z_mid(k):
+        zs[k][0].wait_recv()
+        b_up[k][0:32] = (b_own[k][h_up, 0:32] + b_f[k][0:32].astype(F32)).astype(BF16)
+        b_up[k][32:64] = b_own[k][h_up, 32:64].astype(BF16)
+        zs[k].append(send(b_up[k], b_l[k], {"zh": h_up}))
+        zs[k][1].wait_recv()
+        b_down[k][0:32] = b_own[k][h_down, 0:32].astype(BF16)
+        b_down[k][32:64] = (b_own[k][h_down, 32:64] + b_f[k][32:64].astype(F32)).astype(BF16)
+        zs[k].append(send(b_down[k], b_r[k], {"zh": h_down}))
 
     def z_end(k):
-        for copy in zs[k]:
+        for copy in zs[k] if k == nk - 1 else zs[k][2:]:
             copy.wait_recv()
-        if k == 0:
-            loads["accum"].wait()
         total = b_own[k][zh]
-        for other in (b_l, b_r, b_f):
+        for other in (b_l, b_r, b_f) if k == nk - 1 else (b_l, b_r):
             total = total + other[k][...].astype(F32)
         at, width = chunks[k]
-        wg[:, at : at + width] = accum[:, at : at + width] + total * norm
-        load((2, k), wg.at[:, pl.ds(at, width)], wg_out.at[:, pl.ds(at, width)])
+        wg_out[:, at : at + width] = total
 
     xs = {}
 
@@ -315,7 +334,7 @@
         "enter": enter, "drain": drain, "up": up_grad, "ring": ring_step, "got": arrived,
         "tok_send": tok_send, "tok_pair": tok_pair, "tok_spread": tok_spread, "tok_forward": tok_forward, "tok_turn": tok_turn,
         "w_send": w_send, "w_forward": w_forward, "w_share": w_share, "w_ready": w_ready,
-        "grad_other": grad_other, "grad_own": grad_own, "z_send": z_send, "z_end": z_end,
+        "grad_other": grad_other, "grad_own": grad_own, "z_send": z_send, "z_mid": z_mid, "z_end": z_end,
         "p_begin": p_begin, "p_send": p_send, "p_end": p_end,
     }
     for step, *of in PLAN:
@@ -327,12 +346,8 @@
         def _():
             fin_copy(0, p_fin[0].at[0], other).wait_recv()
 
-    ig[...] = (fin[:, 0].astype(F32) + fin[:, 1].astype(F32)).astype(BF16).reshape(128, 512)
-    load("ig", ig, ig_out)
+    ig_out[...] = fin[...]
     drain()
-    loads["ig"].wait()
-    for k in range(nk):
-        loads[2, k].wait()
     assert len(copies) == n_copies
 
     @pl.when(t != y)
@@ -351,18 +366,15 @@
     norm = 1.0 / math.sqrt(rows * NY * NH * NC)
     ends = (*SPLIT, width)
     chunks = [(at, end - at) for at, end in zip((0, *SPLIT), ends)]
-    n_copies = 14 * len(chunks) + 8 + 4 + 9 + 4 * len(chunks) + 3 * len(TEAMS)
+    n_copies = 14 * len(chunks) + 8 + 4 + 9 + 5 * len(chunks) - 1 + 3 * len(TEAMS)
     dma, vmem = pltpu.SemaphoreType.DMA, pltpu.VMEM
     widths = [w for _, w in chunks]
     sizes = [len(team) for team in TEAMS]
     scratch = [dma((n_copies,)), dma((n_copies,)), dma((NY,)), dma((NX * NL,))]
-    scratch += [dma((3 * len(chunks) + 4,))]
+    scratch += [dma((2 * len(chunks) + 2,))]
     scratch += [
         vmem((width, rows), BF16),
         vmem((width, rows), BF16),
-        vmem((w_rows, width), F32),
-        vmem((w_rows, width), F32),
-        vmem((rows, 512), BF16),
         vmem((rows, 512), BF16),
         vmem((NY, NX, NL, 16, 512), BF16),
         vmem((NC, 256, 1024), BF16),
@@ -372,26 +384,30 @@
     scratch += [vmem((NY, rows, w), BF16) for w in widths]
     for shape, kind in (
         ((NH, 64), BF16), ((NH, 64), BF16), ((NH, 64), F32), ((NH, 64), BF16),
-        ((64,), BF16), ((64,), BF16), ((64,), BF16),
+        ((64,), BF16), ((64,), BF16), ((64,), BF16), ((64,), BF16), ((64,), BF16),
     ):
         scratch += [vmem((*shape, w), kind) for w in widths]
     scratch += [vmem((n * 128, 512), F32) for n in sizes]
     scratch += [vmem((n, NX, 32, 512), BF16) for n in sizes]
     for _ in range(4):
         scratch += [vmem((n, 32, 512), BF16) for n in sizes]
-    return pl.pallas_call(
-        functools.partial(kernel, norm, chunks, n_copies),
+    in_hbm = lambda v: pltpu.with_memory_space_constraint(v, pltpu.HBM)
+    total, parts = pl.pallas_call(
+        functools.partial(kernel, chunks, n_copies),
         out_shape=(
-            jax.ShapeDtypeStruct((w_rows, width), F32),
-            jax.ShapeDtypeStruct((rows, channels // NY), BF16),
+            vmem((w_rows, width), F32),
+            vmem((NX, NL, 32, channels // NY), BF16),
         ),
-        in_specs=[pl.BlockSpec(memory_space=pltpu.HBM)] * 5,
-        out_specs=(pl.BlockSpec(memory_space=pltpu.HBM),) * 2,
+        in_specs=[pl.BlockSpec(memory_space=pltpu.HBM)] * 4,
+        out_specs=(pl.BlockSpec(memory_space=pltpu.VMEM),) * 2,
         scratch_shapes=scratch,
         compiler_params=pltpu.CompilerParams(
-            collective_id=0, has_side_effects=True, vmem_limit_bytes=56 * 1024 * 1024
+            collective_id=0, has_side_effects=True, vmem_limit_bytes=48 * 1024 * 1024
         ),
-    )(tokens, gate_pre.T, hid_grad.T, up_weight, grad_accum)
+    )(*(in_hbm(v) for v in (tokens, gate_pre.T, hid_grad.T, up_weight)))
+    weight_grad = grad_accum + total * norm
+    input_grad = (parts[:, 0].astype(F32) + parts[:, 1].astype(F32)).astype(BF16)
+    return weight_grad, input_grad.reshape(rows, channels // NY)
 
 
 def solution(mesh):

time: 80.1 us -> 77 us (0.961)
  local copies, waits for them, and re-layouts: 2.53 us -> 0.01 us
  Pallas kernels: 76.8 us -> 74.6 us
  other arithmetic: 0 us -> 1.52 us
    unnamed x4 -> x2, local copies, waits for them, and re-layouts: 2.53 us -> 0.01 us
    pallas_call x1, Pallas kernels: 76.8 us -> 74.6 us  [on_device(): pl.pallas_call(functools.partial(kernel, chunks, n_copies), out_shape=(vm...]
    add x0 -> x1, other arithmetic: none -> 0.84 us  [on_device(): weight_grad = grad_accum + total * norm]
where the time goes in v4:
time: 77 us; the launch traced here: 76.8 us
  Pallas kernels  74.6 us (97%)
  other arithmetic  1.52 us (2%)
    pallas_call x1, Pallas kernels, on_device(): pl.pallas_call(functools.partial(kernel, chunks, n_copies), out_shape=(vm...  74.6 us

profile of v4, /device:TPU:1, one launch (start us, length us, event | category | flops | bytes accessed | tf_op | source)
XLA Modules:
  0.0 76.8 jit_solution(13610747286835709804)
XLA Ops:
  0.6 0.0 copy-start
  0.6 74.6 %shard_map.68 = (f32[64,1848]{1,0:T(8,128)S(1)}, bf16[4,2,32,512]{3,2,1,0:T(8,128)(2,1)S(1)}) custom-call(bf16[128,4096]{1,0:T(8,128)(2,1)} %tokens.1, bf16[1848,128]{1,0:T(8,128)(2,1)} %bitcast.3, bf16[1848,128]{1,0:T(8,128)(2,1)} %bitcast.4, bf16[64,1848]{1,0:T(8,128)(2,1)} %w_own.1), custom_call_target="tpu_custom_call" | custom-call | tf_op jit(solution)/shard_map/pallas_call | solution.py:395
  75.3 0.0 copy-done
  75.3 0.8 %multiply_add_fusion = f32[64,1848]{1,0:T(8,128)} fusion(f32[64,1848]{1,0:T(8,128)S(1)} %copy-done, f32[64,1848]{1,0:T(8,128)S(1)} %get-tuple-element.4), kind=kLoop, calls=%fused_computation | loop fusion | flops 236544 | bytes 1419264 | tf_op jit(solution)/shard_map/add | solution.py:408
  76.1 0.7 add_convert_fusion
Async XLA Ops:
  0.6 74.7 %copy-start = (f32[64,1848]{1,0:T(8,128)S(1)}, f32[64,1848]{1,0:T(8,128)}, u32[]{:S(2)}) copy-start(f32[64,1848]{1,0:T(8,128)} %param.9) | copy-start | bytes 1419268

commit v5 on v4

--- a/solution.py
+++ b/solution.py
@@ -13,26 +13,26 @@
 BACK = (0, 2, 1, 4, 3, 6, 5, 7)
 PLUS, MINUS = (0, 2, 4, 6, 7), (0, 1, 3, 5, 7)
 TEAMS = ((0,), (1, 2), (3, 4), (5, 6), (7,))
-SPLIT = (512, 1024, 1536)
+SPLIT = (640, 1152, 1536)
 F32, BF16 = jnp.float32, jnp.bfloat16
 PLAN = (
-    ("up", 0), ("enter",), ("ring", 0, 0, 0), ("w_send",), ("ring", 0, 1, 0), ("tok_send",),
-    ("up", 1), ("up", 2), ("ring", 1, 1, 0), ("ring", 0, 1, 1), ("up", 3), ("ring", 2, 1, 0),
-    ("ring", 1, 0, 0), ("tok_pair",), ("ring", 1, 1, 1), ("ring", 0, 0, 1), ("ring", 0, 1, 2),
-    ("w_forward",), ("ring", 1, 0, 1), ("ring", 2, 0, 0), ("tok_spread",), ("ring", 1, 1, 2),
-    ("ring", 0, 0, 2), ("ring", 1, 0, 2), ("ring", 3, 0, 0), ("w_share",), ("ring", 3, 1, 0),
-    ("ring", 0, 1, 3), ("ring", 1, 1, 3), ("tok_forward",), ("ring", 0, 0, 3), ("w_ready",),
-    ("p_begin", 0), ("p_send", 0), ("ring", 1, 0, 3), ("ring", 2, 0, 1), ("ring", 2, 1, 1),
-    ("p_begin", 1), ("ring", 3, 0, 1), ("ring", 3, 1, 1), ("p_send", 1), ("got", 0, 1, 4),
-    ("tok_turn",), ("got", 0, 0, 4), ("grad_other", 0), ("grad_own", 0), ("got", 1, 1, 4),
-    ("got", 1, 0, 4), ("grad_other", 1), ("ring", 2, 0, 2), ("z_send", 0), ("grad_own", 1),
-    ("ring", 2, 1, 2), ("z_send", 1), ("ring", 3, 1, 2), ("ring", 3, 0, 2), ("p_begin", 2),
-    ("p_send", 2), ("ring", 2, 0, 3), ("z_mid", 0), ("ring", 2, 1, 3), ("p_end", 1), ("p_begin", 3),
-    ("ring", 3, 1, 3), ("z_mid", 1), ("ring", 3, 0, 3), ("p_send", 3), ("p_end", 0),
-    ("got", 2, 0, 4), ("got", 2, 1, 4), ("grad_other", 2), ("grad_own", 2), ("p_begin", 4),
-    ("got", 3, 0, 4), ("got", 3, 1, 4), ("grad_other", 3), ("z_send", 2), ("p_send", 4),
-    ("p_end", 2), ("grad_own", 3), ("z_send", 3), ("p_end", 3), ("p_end", 4), ("drain",),
-    ("z_mid", 2), ("z_end", 0), ("z_end", 1), ("z_end", 3), ("z_end", 2),
+    ("up", 0), ("enter",), ("ring", 0, 0, 0), ("w_send",), ("tok_send",), ("up", 1), ("up", 2),
+    ("ring", 2, 1, 0), ("up", 3), ("ring", 3, 0, 0), ("ring", 0, 1, 0), ("ring", 2, 0, 0),
+    ("ring", 1, 0, 0), ("ring", 0, 0, 1), ("tok_pair",), ("ring", 0, 1, 1), ("ring", 2, 1, 1),
+    ("ring", 2, 0, 1), ("w_forward",), ("ring", 0, 0, 2), ("ring", 1, 1, 0), ("tok_spread",),
+    ("ring", 0, 1, 2), ("ring", 2, 1, 2), ("ring", 2, 0, 2), ("ring", 0, 0, 3), ("ring", 3, 1, 0),
+    ("w_share",), ("tok_forward",), ("w_ready",), ("p_begin", 0), ("p_send", 0), ("ring", 0, 1, 3),
+    ("ring", 1, 1, 1), ("ring", 1, 0, 1), ("ring", 2, 0, 3), ("ring", 3, 0, 1), ("ring", 2, 1, 3),
+    ("p_begin", 1), ("ring", 3, 1, 1), ("tok_turn",), ("got", 0, 0, 4), ("got", 0, 1, 4),
+    ("grad_other", 0), ("p_send", 1), ("ring", 1, 1, 2), ("grad_own", 0), ("z_send", 0),
+    ("ring", 1, 0, 2), ("p_begin", 2), ("ring", 3, 0, 2), ("got", 2, 1, 4), ("got", 2, 0, 4),
+    ("grad_other", 2), ("ring", 3, 1, 2), ("p_send", 2), ("grad_own", 2), ("z_send", 2),
+    ("ring", 1, 1, 3), ("z_mid", 0), ("ring", 1, 0, 3), ("p_begin", 3), ("ring", 3, 0, 3),
+    ("p_end", 0), ("ring", 3, 1, 3), ("p_end", 1), ("p_send", 3), ("z_mid", 2), ("p_end", 2),
+    ("got", 1, 1, 4), ("got", 1, 0, 4), ("grad_other", 1), ("grad_own", 1), ("p_begin", 4),
+    ("got", 3, 1, 4), ("got", 3, 0, 4), ("grad_other", 3), ("z_send", 1), ("p_send", 4),
+    ("grad_own", 3), ("z_send", 3), ("p_end", 3), ("z_end", 0), ("p_end", 4), ("drain",),
+    ("z_end", 2), ("z_mid", 1), ("z_end", 3), ("z_end", 1),
 )
 
 

time: 77 us -> 77.3 us (level)
  no operation moved by 1% of the time
where the time goes in v5:
time: 77.3 us; the launch traced here: 77.2 us
  Pallas kernels  75 us (97%)
  other arithmetic  1.52 us (2%)
    pallas_call x1, Pallas kernels, on_device(): pl.pallas_call(functools.partial(kernel, chunks, n_copies), out_shape=(vm...  75 us

profile of v5, /device:TPU:1, one launch (start us, length us, event | category | flops | bytes accessed | tf_op | source)
XLA Modules:
  0.0 77.2 jit_solution(14258165930129264924)
XLA Ops:
  0.6 0.0 copy-start
  0.6 75.0 %shard_map.68 = (f32[64,1848]{1,0:T(8,128)S(1)}, bf16[4,2,32,512]{3,2,1,0:T(8,128)(2,1)S(1)}) custom-call(bf16[128,4096]{1,0:T(8,128)(2,1)} %tokens.1, bf16[1848,128]{1,0:T(8,128)(2,1)} %bitcast.3, bf16[1848,128]{1,0:T(8,128)(2,1)} %bitcast.4, bf16[64,1848]{1,0:T(8,128)(2,1)} %w_own.1), custom_call_target="tpu_custom_call" | custom-call | tf_op jit(solution)/shard_map/pallas_call | solution.py:395
  75.7 0.0 copy-done
  75.7 0.8 %multiply_add_fusion = f32[64,1848]{1,0:T(8,128)} fusion(f32[64,1848]{1,0:T(8,128)S(1)} %copy-done, f32[64,1848]{1,0:T(8,128)S(1)} %get-tuple-element.4), kind=kLoop, calls=%fused_computation | loop fusion | flops 236544 | bytes 1419264 | tf_op jit(solution)/shard_map/add | solution.py:408
  76.5 0.7 add_convert_fusion
Async XLA Ops:
  0.6 75.0 %copy-start = (f32[64,1848]{1,0:T(8,128)S(1)}, f32[64,1848]{1,0:T(8,128)}, u32[]{:S(2)}) copy-start(f32[64,1848]{1,0:T(8,128)} %param.9) | copy-start | bytes 1419268
